TPU v7x, 32 devices: a whole 2x2x4 slice. The times are simulated.
32 devices in a mesh: fsdp: 4 (over z), cb: 8 (over y, x, core).
Axes of the slice: x: 2, y: 2, z: 4, core: 2. Of those that a mesh axis runs over, the one named last changes fastest.
Arguments:
- frames_in: bfloat16 [4, 256, 6144], P('fsdp', 'cb'), may hold values from -6 to 6
- valid_len: int32 [4], P('fsdp'), may hold values from 128 to 256
- tokens: int32 [4, 8, 256], P('fsdp', 'cb'), may hold values from 0 to 2047
- t_gain: float32 [6144], replicated, may hold values from 0.25 to 1.75
- w_qkv: bfloat16 [6144, 12288], P('fsdp', 'cb'), as said below
- w_out: bfloat16 [4096, 6144], P('cb', 'fsdp'), may hold values from -0.09375 to 0.09375
- h_gain: float32 [6144], replicated, may hold values from 0.25 to 1.75
- d_in: bfloat16 [8, 6144, 1024], P('cb'), may hold values from -0.078125 to 0.078125
- d_embed: bfloat16 [8, 2048, 1024], P('cb'), may hold values from -6 to 6
- d_gain: float32 [8, 1024], P('cb'), may hold values from 0.25 to 1.75
- d_qkv: bfloat16 [8, 1024, 3072], P('cb'), as said below
Outputs:
- depth_mix: bfloat16 [4, 8, 256, 1024], P('fsdp', 'cb')
Inputs may be any that keep to these rules, and one draw needn't show every extreme that they name: `w_qkv`: every entry of the temporal projections has magnitude at most 31 / sqrt(6144). `d_qkv`: every entry of the depth projections has magnitude at most 31 / sqrt(1024).
All inputs are finite; a program needn't handle non-finite values.
Results may differ from a plain program's by a relative error of at most 0.012.
Values may be sent and summed in bfloat16 or wider, within the bound.
A program may use at most 128 MiB of HBM per device.

v0:
```python
import math

import jax
import jax.numpy as jnp
from jax import lax
from jax.sharding import PartitionSpec as P

HEAD = 128
DHEAD = 64


EPS = 1e-05
NEG = -1e30


def rms_scale(values, gain):
    mean_sq = jnp.mean(values * values, axis=-1, keepdims=True)
    return values * lax.rsqrt(mean_sq + EPS) * gain


def body(frames_in, valid_len, tokens, t_gain, w_qkv, w_out, h_gain, d_in, d_embed, d_gain, d_qkv):
    gathered = lax.all_gather(frames_in, "cb", axis=1, tiled=True)[0]
    length = gathered.shape[0]
    normed = rms_scale(gathered.astype(jnp.float32), t_gain).astype(jnp.bfloat16)
    every = lax.all_to_all(normed, "fsdp", split_axis=1, concat_axis=0, tiled=True)
    packed = lax.psum_scatter(
        jnp.dot(every, w_qkv, preferred_element_type=jnp.float32),
        "fsdp",
        scatter_dimension=0,
        tiled=True,
    )
    packed = packed.astype(jnp.bfloat16).reshape(length, -1, 3, HEAD)
    query = packed[:, :, 0]
    keys = packed[:, :, 1]
    values = packed[:, :, 2]
    scores = jnp.einsum(
        "ihe,jhe->hij", query, keys, preferred_element_type=jnp.float32
    ) / math.sqrt(HEAD)
    rows = lax.broadcasted_iota(jnp.int32, (length, length), 0)
    cols = lax.broadcasted_iota(jnp.int32, (length, length), 1)
    allowed = ((cols <= rows) & (cols < valid_len[0]))[None]
    scores = jnp.where(allowed, scores, NEG)
    top = jnp.max(scores, axis=-1, keepdims=True)
    expo = jnp.where(allowed, jnp.exp(scores - top), 0.0)
    probs = (expo / jnp.sum(expo, axis=-1, keepdims=True)).astype(jnp.bfloat16)
    mixed = jnp.einsum("hij,jhe->ihe", probs, values, preferred_element_type=jnp.float32)
    mixed = mixed.astype(jnp.bfloat16).reshape(length, -1)
    partial_out = jnp.dot(
        mixed, lax.all_gather(w_out, "fsdp", axis=1, tiled=True), preferred_element_type=jnp.float32
    )
    total = lax.psum(partial_out, "cb")
    hidden = gathered.astype(jnp.float32) + total
    hnorm = rms_scale(hidden, h_gain).astype(jnp.bfloat16)
    lifted = jnp.dot(hnorm, d_in[0], preferred_element_type=jnp.float32)
    lifted = lifted + jnp.take(d_embed[0], tokens[0, 0], axis=0).astype(jnp.float32)
    dnorm = rms_scale(lifted, d_gain[0]).astype(jnp.bfloat16)
    depth_all = jnp.dot(dnorm, d_qkv[0], preferred_element_type=jnp.float32).astype(jnp.bfloat16)
    inner = d_in.shape[2]
    dquery = depth_all[:, :inner].reshape(length, -1, DHEAD)
    head_count = dquery.shape[1]
    pairs = depth_all[None, :, inner:]
    section = lax.axis_index("cb")
    piece = lax.all_gather(pairs, "cb", axis=0, tiled=True)
    best = jnp.full((length, head_count), NEG, jnp.float32)
    count = piece.shape[0]
    dkeys = piece[:, :, :inner].reshape(count, length, head_count, DHEAD)
    dvals = piece[:, :, inner:].reshape(count, length, head_count, DHEAD)
    dscore = jnp.einsum(
        "ihe,nihe->nih", dquery, dkeys, preferred_element_type=jnp.float32
    ) / math.sqrt(DHEAD)
    order = lax.broadcasted_iota(jnp.int32, (count, 1, 1), 0)
    keep = (order <= section) & (order >= 0)
    dscore = jnp.where(keep, dscore, NEG)
    fresh = jnp.maximum(best, jnp.max(dscore, axis=0))
    weights = jnp.where(keep, jnp.exp(dscore - fresh), 0.0)
    total = jnp.sum(weights, axis=0)
    accum = jnp.einsum("nih,nihe->ihe", weights, dvals.astype(jnp.float32))
    best, total, accum = (fresh, total, accum)
    result = (accum / total[..., None]).reshape(length, inner).astype(jnp.bfloat16)
    return result[None, None]


def solution(mesh):
    placed = (
        P("fsdp", "cb", None),
        P("fsdp"),
        P("fsdp", "cb", None),
        P(),
        P("fsdp", "cb"),
        P("cb", "fsdp"),
        P(),
        P("cb", None, None),
        P("cb", None, None),
        P("cb", None),
        P("cb", None, None),
    )
    return jax.shard_map(
        body, mesh=mesh, in_specs=placed, out_specs=P("fsdp", "cb", None, None), check_vma=False
    )
```

profile of v0, /device:TPU:0, one launch (start us, length us, event | category | flops | bytes accessed | tf_op | source)
XLA Modules:
  0.0 583.9 jit_solution(9148326716170234945)
XLA Ops:
  8.1 36.2 %all-gather.5.cloned.1.call-done = bf16[1,256,6144]{2,1,0:T(8,128)(2,1)} async-done(((bf16[1,32,6144]{2,1,0:T(8,128)(2,1)}), bf16[1,256,6144]{2,1,0:T(8,128)(2,1)}) %all-gather.5.cloned.1.call-update) | async-done | bytes 3145744 | tf_op jit(solution)/shard_map/all_gather | solution.py:22
  44.3 2.6 fusion.5
  46.9 8.0 %reshape.146 = f32[256,4,1536]{2,1,0:T(4,128)} reshape(bf16[1,256,6144]{2,1,0:T(8,128)(2,1)} %all-gather.5.cloned.1.call-done) | data formatting | bytes 9437184 | tf_op jit(solution)/shard_map/convert_element_type | solution.py:52
  54.9 4.8 fusion.7
  59.7 75.5 %all_to_all.16 = bf16[256,4,1536]{2,0,1:T(8,128)(2,1)S(1)} all-to-all(bf16[256,4,1536]{2,0,1:T(8,128)(2,1)S(1)} %fusion.7), channel_id=1, replica_groups=mesh['fsdp'=4,'cb'=8] {'fsdp'}, dimensions={1} | all-to-all | bytes 6291456 | tf_op jit(solution)/shard_map/all_to_all | solution.py:25
  135.1 9.2 %fusion.38 = f32[1024,1536]{1,0:T(8,128)} fusion(bf16[1024,1536]{1,0:T(8,128)(2,1)S(1)} %bitcast.105, bf16[1536,1536]{1,0:T(8,128)(2,1)} %param.15), kind=kOutput, calls=%fused_computation.64 | convolution fusion | flops 4831838208 | bytes 14155776 | tf_op jit(solution)/shard_map/dot_general | solution.py:27
  145.9 107.5 %reduce-scatter.2.cloned.1.call-done = f32[256,1536]{1,0:T(8,128)} async-done(((f32[1024,1536]{1,0:T(8,128)}), f32[256,1536]{1,0:T(8,128)}) %reduce-scatter.2.cloned.1.call-update) | async-done | bytes 1572880 | tf_op jit(solution)/shard_map/reduce_scatter | solution.py:26
  253.4 1.5 convert_element_type.60
  255.9 0.8 convolution_convert_fusion
  256.7 114.2 %all-gather.7.cloned.1.call-done = bf16[512,6144]{1,0:T(8,128)(2,1)} async-done(((bf16[512,1536]{1,0:T(8,128)(2,1)}), bf16[512,6144]{1,0:T(8,128)(2,1)}) %all-gather.7.cloned.1.call-update) | async-done | bytes 6291472 | tf_op jit(solution)/shard_map/all_gather | solution.py:49
  370.9 7.3 %fusion.39 = f32[256,6144]{1,0:T(8,128)} fusion(bf16[256,512]{0,1:T(8,128)(2,1)S(1)} %bitcast.109, bf16[512,6144]{1,0:T(8,128)(2,1)} %all-gather.7.cloned.1.call-done), kind=kOutput, calls=%fused_computation.65 | convolution fusion | flops 1610612736 | bytes 12845056 | tf_op jit(solution)/shard_map/dot_general | solution.py:48
  378.9 5.3 gather_fusion
  384.2 96.5 %all-reduce.2.cloned.1.call-done = f32[256,6144]{1,0:T(8,128)} async-done(((f32[256,6144]{1,0:T(8,128)}), f32[256,6144]{1,0:T(8,128)}) %all-reduce.2.cloned.1.call-update) | async-done | bytes 6291472 | tf_op jit(solution)/shard_map/psum | solution.py:51
  480.8 3.8 multiply_reduce_fusion.2
  485.4 7.0 %multiply_reduce_fusion.3 = (f32[256]{0:T(256)S(1)}, f32[256,1024]{1,0:T(8,128)S(1)}) fusion(bf16[256,1024]{1,0:T(8,128)(2,1)S(1)} %copy-done.2, pred[256]{0:T(512)(128)(4,1)S(1)} %compare_and_fusion, bf16[1,6144,1024]{2,1,0:T(8,128)(2,1)} %param.18, f32[256,6144]{1,0:T(8,128)S(1)} %copy-done.1, bf16[1,256,6144]{2,1,0:T(8,128)(2,1)S(1)} %copy-done, ...), kind=kOutput, calls=%fused_computation.28 | convolution fusion | flops 3230400256 | bytes 23619840 | tf_op jit(solution)/shard_map/dot_general | solution.py:54
  492.4 1.9 fusion.8
  494.3 1.2 slice.33
  495.9 54.3 %all-gather.9.cloned.1.call-done = bf16[2048,2048]{1,0:T(8,128)(2,1)} async-done(((bf16[256,2048]{1,0:T(8,128)(2,1)}), bf16[2048,2048]{1,0:T(8,128)(2,1)}) %all-gather.9.cloned.1.call-update) | async-done | bytes 8388624 | tf_op jit(solution)/shard_map/all_gather | solution.py:63
  550.2 5.9 %fusion.36 = (bf16[8,256,1024]{2,1,0:T(8,128)(2,1)}, bf16[8,256,1024]{2,1,0:T(8,128)(2,1)}) fusion(bf16[8,256,2048]{2,1,0:T(8,128)(2,1)} %bitcast.103), kind=kLoop, calls=%fused_computation.62 | loop fusion | bytes 16777216 | tf_op jit(solution)/shard_map/slice | solution.py:66
  556.1 6.4 %copy.52 = bf16[8,256,1024]{1,2,0:T(8,128)(2,1)} copy(bf16[8,256,1024]{2,1,0:T(8,128)(2,1)} %get-tuple-element.5) | data formatting | bytes 8388608
  562.5 3.6 multiply_reduce_fusion.1
  566.4 6.4 %copy.53 = bf16[8,256,1024]{1,2,0:T(8,128)(2,1)} copy(bf16[8,256,1024]{2,1,0:T(8,128)(2,1)} %get-tuple-element.6) | data formatting | bytes 8388608
  572.8 3.4 multiply_reduce_fusion
  576.4 1.0 copy.35
  (46 shorter events, 5.5 us)
Async XLA Ops:
  6.5 37.8 %all-gather.5.cloned.1.call-start = ((), (), s32[]{:S(2)}) async-start(), calls=%async_computation.2 | async-start | bytes 3538944 | tf_op jit(solution)/shard_map/all_gather | solution.py:22
  7.3 246.2 %reduce-scatter.2.cloned.1.call-start = ((), (), s32[]{:S(2)}) async-start(), calls=%async_computation.3 | async-start | bytes 7864320 | tf_op jit(solution)/shard_map/reduce_scatter | solution.py:26
  144.4 226.5 %all-gather.7.cloned.1.call-start = ((), (), s32[]{:S(2)}) async-start(), calls=%async_computation.4 | async-start | bytes 7864320 | tf_op jit(solution)/shard_map/all_gather | solution.py:49
  145.1 335.6 %all-reduce.2.cloned.1.call-start = ((), (), s32[]{:S(2)}) async-start(), calls=%async_computation.5 | async-start | bytes 12582912 | tf_op jit(solution)/shard_map/psum | solution.py:51
  378.2 0.7 copy-start.3
  378.2 102.5 %copy-start = (bf16[1,256,6144]{2,1,0:T(8,128)(2,1)S(1)}, bf16[1,256,6144]{2,1,0:T(8,128)(2,1)}, u32[]{:S(2)}) copy-start(bf16[1,256,6144]{2,1,0:T(8,128)(2,1)} %all-gather.5.cloned.1.call-done) | copy-start | bytes 9437188
  378.2 171.9 %all-gather.9.cloned.1.call-start = ((), (), s32[]{:S(2)}) async-start(), calls=%async_computation.6 | async-start | bytes 9437184 | tf_op jit(solution)/shard_map/all_gather | solution.py:63
  378.9 105.7 %copy-start.4 = (f32[6144]{0:T(1024)S(1)}, f32[6144]{0:T(1024)}, u32[]{:S(2)}) copy-start(f32[6144]{0:T(1024)} %param.17) | copy-start | bytes 73732
  480.7 4.6 copy-start.1
  480.7 4.7 copy-start.2
  480.7 11.7 %slice-start = ((s8[6291456]{0:T(1024)(128)(4,1)}), s8[4194304]{0:T(1024)(128)(4,1)S(1)}, s32[]{:S(2)}) async-start(s8[6291456]{0:T(1024)(128)(4,1)} %bitcast.112), calls=%async_computation.7 | async-start | bytes 8388608
  485.4 7.0 %slice-start.1 = ((s8[6291456]{0:T(1024)(128)(4,1)}), s8[2097152]{0:T(1024)(128)(4,1)S(1)}, s32[]{:S(2)}) async-start(s8[6291456]{0:T(1024)(128)(4,1)} %bitcast.112), calls=%async_computation.8 | async-start | bytes 4194304
  485.4 7.0 %copy-start.5 = (f32[1,1024]{1,0:T(1,128)S(1)}, f32[1,1024]{1,0:T(1,128)}, u32[]{:S(2)}) copy-start(f32[1,1024]{1,0:T(1,128)} %param.20) | copy-start | bytes 12292
Sparse Core Ops, SparseCore 0:
  9.2 35.0 all-gather.4
  144.5 108.8 reduce-scatter.1
  255.0 115.8 all-gather.6
  378.3 102.3 all-reduce.1
  495.6 54.4 all-gather.8
where the time goes:
time: 585 us; the launch traced here: 584 us
  waiting for transfers between devices  410 us (70%)
  blocking collectives  75.5 us (13%)
  local copies, waits for them, and re-layouts  36.8 us (6%)
  matrix products  26.8 us (5%)
  other arithmetic  20.3 us (3%)
  between operations  14 us (2%)
    all_gather x1, waiting for transfers between devices, body(): lax.all_gather(w_out, 'fsdp', axis=1, tiled=True)  114 us
    reduce_scatter x1, waiting for transfers between devices, body(): lax.psum_scatter(jnp.dot(every, w_qkv, preferred_element_type=jnp.float32...  108 us
    psum x1, waiting for transfers between devices, body(): total = lax.psum(partial_out, 'cb')  96.5 us
    all_to_all x1, blocking collectives, body(): lax.all_to_all(normed, 'fsdp', split_axis=1, concat_axis=0, tiled=True)  75.5 us
    all_gather x1, waiting for transfers between devices, body(): piece = lax.all_gather(pairs, 'cb', axis=0, tiled=True)  54.3 us
    all_gather x1, waiting for transfers between devices, body(): gathered = lax.all_gather(frames_in, 'cb', axis=1, tiled=True)[0]  36.2 us
    unnamed x18, local copies, waits for them, and re-layouts  14.1 us
  transfers between devices with their start and end apart: 5, of which 5 were waited for; matrix products, arithmetic and copies ran while one was open for 2% of the time, Pallas kernels for 0%

commit v1 on v0

v1 whole, which is shorter than its diff:
```python
import functools
import math

import jax
import jax.numpy as jnp
from jax import lax
from jax.experimental import pallas as pl
from jax.experimental.pallas import tpu as pltpu
from jax.sharding import PartitionSpec as P

HEAD = 128
DHEAD = 64


EPS = 1e-05
NEG = -1e30


def rms_scale(values, gain):
    mean_sq = jnp.mean(values * values, axis=-1, keepdims=True)
    return values * lax.rsqrt(mean_sq + EPS) * gain


MESH = pl.DeviceIdType.MESH
VMEM_LIMIT = 56 * 1024 * 1024


def entry_barrier(seqs, chips, f, chip, core):
    barrier = pltpu.get_barrier_semaphore()
    for d in range(1, seqs):
        pl.semaphore_signal(barrier, inc=1, device_id={"fsdp": lax.rem(f + d, seqs)}, device_id_type=MESH)
    for e in range(1, chips):
        peer = lax.rem(chip + e, chips) * 2 + core
        pl.semaphore_signal(barrier, inc=1, device_id={"cb": peer}, device_id_type=MESH)
    pl.semaphore_signal(barrier, inc=1, device_id={"cb": chip * 2 + 1 - core}, device_id_type=MESH)
    pl.semaphore_wait(barrier, seqs + chips - 1)


def send(src, dst, send_sem, recv_sem, device):
    return pltpu.make_async_remote_copy(
        src_ref=src, dst_ref=dst, send_sem=send_sem, recv_sem=recv_sem,
        device_id=device, device_id_type=MESH,
    )


def qkv_kernel(
    seqs, chips, frames, gain, w_hbm, out, normed, gat, w, part, from_left, from_right,
    z_send, z_recv, c_send, c_recv, b_send, b_recv, right_send, right_recv, left_send, left_recv, w_sem,
):
    f = lax.axis_index("fsdp")
    me = lax.axis_index("cb")
    chip, core = lax.div(me, 2), lax.rem(me, 2)
    sibling = chip * 2 + 1 - core
    few, wide = frames.shape
    width = wide // seqs
    length = out.shape[0]
    cols = out.shape[1]
    last = seqs - 1
    order = []
    for k in range(seqs):
        order.append(last - k // 2 if k % 2 == 0 else k // 2)

    load = pltpu.make_async_copy(w_hbm, w, w_sem)
    load.start()
    entry_barrier(seqs, chips, f, chip, core)
    total = jnp.zeros((few, 1), jnp.float32)
    for b in range(seqs):
        block = frames[:, b * width : (b + 1) * width].astype(jnp.float32)
        total = total + jnp.sum(block * block, axis=-1, keepdims=True)
    scale = lax.rsqrt(total / wide + EPS)
    for b in range(seqs):
        block = frames[:, b * width : (b + 1) * width].astype(jnp.float32)
        normed[b] = (block * scale * gain[:, b * width : (b + 1) * width]).astype(jnp.bfloat16)
    gat[me, f] = normed[f]

    def along_z(t):
        return send(normed.at[t], gat.at[me, f], z_send.at[t], z_recv.at[f], {"fsdp": t})

    for t in order:
        @pl.when(t != f)
        def _():
            along_z(t).start()

    def to_chip(s, e):
        peer = lax.rem(chip + e, chips) * 2 + core
        return send(gat.at[me, s], gat.at[me, s], c_send.at[s, e], c_recv.at[s, e], {"cb": peer})

    def to_sibling(s, e):
        source = lax.rem(chip - e + chips, chips) * 2 + core
        return send(gat.at[source, s], gat.at[source, s], b_send.at[s, e], b_recv.at[s, e], {"cb": sibling})

    for s in order:
        @pl.when(s != f)
        def _():
            send(normed.at[s], gat.at[me, s], z_send.at[s], z_recv.at[s], {"fsdp": s}).wait_recv()

        for e in range(1, chips):
            to_chip(s, e).start()
        to_sibling(s, 0).start()

    def to_right(t):
        return send(part.at[t], from_left.at[t], right_send.at[t], right_recv.at[t], {"fsdp": lax.rem(f + 1, seqs)})

    def to_left(t):
        return send(part.at[t], from_right.at[t], left_send.at[t], left_recv.at[t], {"fsdp": lax.rem(f + last, seqs)})

    load.wait()
    tile = 256
    for s in order:
        for e in range(1, chips):
            source = lax.rem(chip - e + chips, chips) * 2 + core
            send(gat.at[source, s], gat.at[source, s], c_send.at[s, e], c_recv.at[s, e], {"cb": sibling}).wait_recv()
            to_sibling(s, e).start()
        for e in range(chips):
            source = lax.rem(chip - e + chips, chips) * 2 + 1 - core
            send(gat.at[source, s], gat.at[source, s], b_send.at[s, e], b_recv.at[s, e], {"cb": sibling}).wait_recv()

        def multiply(step, carry):
            at = pl.ds(pl.multiple_of(step * tile, tile), tile)
            lhs = gat[:, s].reshape(length, width)
            part[s, :, at] = jnp.dot(lhs, w[:, at], preferred_element_type=jnp.float32).astype(jnp.bfloat16)
            return carry

        lax.fori_loop(0, cols // tile, multiply, 0)
        if s > 0:
            @pl.when(f == 0)
            def _():
                to_right(s).start()
        if s < last:
            @pl.when(f == last)
            def _():
                to_left(s).start()

    def add(target, t, other):
        def rows(step, carry):
            at = pl.ds(pl.multiple_of(step * 32, 32), 32)
            target[t, at] = (target[t, at].astype(jnp.float32) + other[t, at].astype(jnp.float32)).astype(jnp.bfloat16)
            return carry

        lax.fori_loop(0, length // 32, rows, 0)

    for k in range(1, seqs):
        t = seqs - k

        @pl.when((f > 0) & (t > f))
        def _():
            to_right(t).wait_recv()
            add(part, t, from_left)
            to_right(t).start()

        u = k - 1

        @pl.when((f < last) & (u < f))
        def _():
            to_left(u).wait_recv()
            add(part, u, from_right)
            to_left(u).start()

    @pl.when(f > 0)
    def _():
        to_right(f).wait_recv()
        add(part, f, from_left)

    @pl.when(f < last)
    def _():
        to_left(f).wait_recv()
        add(part, f, from_right)

    def finish(step, carry):
        at = pl.ds(pl.multiple_of(step * 32, 32), 32)
        out[at] = part[f, at]
        return carry

    lax.fori_loop(0, length // 32, finish, 0)

    for s in range(seqs):
        @pl.when(s != f)
        def _():
            along_z(s).wait_send()

        @pl.when(s > f)
        def _():
            to_right(s).wait_send()

        @pl.when(s < f)
        def _():
            to_left(s).wait_send()

        for e in range(chips):
            to_sibling(s, e).wait_send()
            if e > 0:
                to_chip(s, e).wait_send()


def temporal_qkv(seqs, parts, own, gain, w_qkv):
    few, wide = own.shape
    width, cols = w_qkv.shape
    chips = parts // 2
    length = parts * few
    dma = pltpu.SemaphoreType.DMA
    vmem = pl.BlockSpec(memory_space=pltpu.VMEM)
    return pl.pallas_call(
        functools.partial(qkv_kernel, seqs, chips),
        out_shape=jax.ShapeDtypeStruct((length, cols), jnp.bfloat16),
        in_specs=[vmem, vmem, pl.BlockSpec(memory_space=pl.ANY)],
        out_specs=vmem,
        scratch_shapes=[
            pltpu.VMEM((seqs, few, width), jnp.bfloat16),
            pltpu.VMEM((parts, seqs, few, width), jnp.bfloat16),
            pltpu.VMEM((width, cols), jnp.bfloat16),
            pltpu.VMEM((seqs, length, cols), jnp.bfloat16),
            pltpu.VMEM((seqs, length, cols), jnp.bfloat16),
            pltpu.VMEM((seqs, length, cols), jnp.bfloat16),
            dma((seqs,)), dma((seqs,)),
            dma((seqs, chips)), dma((seqs, chips)),
            dma((seqs, chips)), dma((seqs, chips)),
            dma((seqs,)), dma((seqs,)), dma((seqs,)), dma((seqs,)),
            dma,
        ],
        compiler_params=pltpu.CompilerParams(
            collective_id=0, has_side_effects=True, vmem_limit_bytes=VMEM_LIMIT
        ),
        cost_estimate=pl.CostEstimate(
            flops=2 * seqs * length * width * cols, bytes_accessed=2 * width * cols, transcendentals=0
        ),
    )(own, gain, w_qkv)


def out_kernel(
    seqs, chips, mixed, w, own, gain, out, gath, part, from_sib, acc, from_chip, total, cols, hid, gat,
    z_send, z_recv, s_send, s_recv, c_send, c_recv, t_send, t_recv, g_send, g_recv, b_send, b_recv, o_sem,
):
    f = lax.axis_index("fsdp")
    me = lax.axis_index("cb")
    chip, core = lax.div(me, 2), lax.rem(me, 2)
    sibling = chip * 2 + 1 - core
    few, wide = own.shape
    width = wide // seqs
    length = mixed.shape[0]
    tile = 256
    entry_barrier(seqs, chips, f, chip, core)

    def along_z(d):
        return send(mixed, gath.at[f], z_send.at[d], z_recv.at[d], {"fsdp": lax.rem(f + d, seqs)})

    for d in range(1, seqs):
        along_z(d).start()
    gath[f] = mixed[...]

    def to_sibling(s, d):
        return send(part.at[1 - core, s], from_sib.at[s], s_send.at[d], s_recv.at[d], {"cb": sibling})

    def to_chip(s, d, e):
        q = lax.rem(chip + e, chips)
        return send(acc.at[s, q], from_chip.at[s, e], c_send.at[d, e], c_recv.at[d, e], {"cb": q * 2 + core})

    def to_seq(s, d):
        return send(total.at[s], cols.at[f], t_send.at[d], t_recv.at[d], {"fsdp": s})

    for d in range(seqs):
        s = lax.rem(f - d + seqs, seqs)
        if d > 0:
            along_z(d).wait_recv()

        def multiply(step, carry):
            at = pl.ds(pl.multiple_of(step * tile, tile), tile)
            value = jnp.dot(gath[s], w[:, at], preferred_element_type=jnp.float32).astype(jnp.bfloat16)
            value = value.reshape(chips, 2, few, tile)
            part[0, s, :, :, at] = value[:, 0]
            part[1, s, :, :, at] = value[:, 1]
            return carry

        lax.fori_loop(0, width // tile, multiply, 0)
        to_sibling(s, d).start()

    for d in range(seqs):
        s = lax.rem(f - d + seqs, seqs)
        to_sibling(s, d).wait_recv()

        def pair(q, carry):
            acc[s, q] = (
                part[core, s, q].astype(jnp.float32) + from_sib[s, q].astype(jnp.float32)
            ).astype(jnp.bfloat16)
            return carry

        lax.fori_loop(0, chips, pair, 0)
        for e in range(1, chips):
            to_chip(s, d, e).start()

    for d in range(seqs):
        s = lax.rem(f - d + seqs, seqs)
        value = acc[s, chip].astype(jnp.float32)
        for e in range(1, chips):
            to_chip(s, d, e).wait_recv()
            value = value + from_chip[s, e].astype(jnp.float32)
        if d > 0:
            total[s] = value.astype(jnp.bfloat16)
            to_seq(s, d).start()
        else:
            cols[f] = value.astype(jnp.bfloat16)

    for d in range(1, seqs):
        to_seq(lax.rem(f - d + seqs, seqs), d).wait_recv()
    square = jnp.zeros((few, 1), jnp.float32)
    for b in range(seqs):
        at = slice(b * width, (b + 1) * width)
        block = own[:, at].astype(jnp.float32) + cols[b].astype(jnp.float32)
        hid[:, at] = block
        square = square + jnp.sum(block * block, axis=-1, keepdims=True)
    scale = lax.rsqrt(square / wide + EPS)
    for b in range(seqs):
        at = slice(b * width, (b + 1) * width)
        gat[me, :, at] = (hid[:, at] * scale * gain[:, at]).astype(jnp.bfloat16)

    def share(e):
        peer = lax.rem(chip + e, chips) * 2 + core
        return send(gat.at[me], gat.at[me], g_send.at[e], g_recv.at[e], {"cb": peer})

    def forward(e):
        source = lax.rem(chip - e + chips, chips) * 2 + core
        return send(gat.at[source], gat.at[source], b_send.at[e], b_recv.at[e], {"cb": sibling})

    for e in range(1, chips):
        share(e).start()
    forward(0).start()
    for e in range(1, chips):
        share(e).wait_recv()
        forward(e).start()
    for e in range(chips):
        forward(e).wait_recv()
    keep = pltpu.make_async_copy(gat, out, o_sem)
    keep.start()
    for d in range(seqs):
        s = lax.rem(f - d + seqs, seqs)
        to_sibling(s, d).wait_send()
        for e in range(1, chips):
            to_chip(s, d, e).wait_send()
        if d > 0:
            along_z(d).wait_send()
            to_seq(s, d).wait_send()
    for e in range(chips):
        forward(e).wait_send()
        if e > 0:
            share(e).wait_send()
    keep.wait()


def temporal_out(seqs, parts, mixed, w_out, own, gain):
    few, wide = own.shape
    depth, width = w_out.shape
    chips = parts // 2
    length = parts * few
    dma = pltpu.SemaphoreType.DMA
    vmem = pl.BlockSpec(memory_space=pltpu.VMEM)
    bf16 = jnp.bfloat16
    return pl.pallas_call(
        functools.partial(out_kernel, seqs, chips),
        out_shape=jax.ShapeDtypeStruct((parts, few, wide), bf16),
        in_specs=[vmem] * 4,
        out_specs=pl.BlockSpec(memory_space=pl.ANY),
        scratch_shapes=[
            pltpu.VMEM((seqs, length, depth), bf16),
            pltpu.VMEM((2, seqs, chips, few, width), bf16),
            pltpu.VMEM((seqs, chips, few, width), bf16),
            pltpu.VMEM((seqs, chips, few, width), bf16),
            pltpu.VMEM((seqs, chips, few, width), bf16),
            pltpu.VMEM((seqs, few, width), bf16),
            pltpu.VMEM((seqs, few, width), bf16),
            pltpu.VMEM((few, wide), jnp.float32),
            pltpu.VMEM((parts, few, wide), bf16),
            dma((seqs,)), dma((seqs,)),
            dma((seqs,)), dma((seqs,)),
            dma((seqs, chips)), dma((seqs, chips)),
            dma((seqs,)), dma((seqs,)),
            dma((chips,)), dma((chips,)),
            dma((chips,)), dma((chips,)),
            dma,
        ],
        compiler_params=pltpu.CompilerParams(
            collective_id=1, has_side_effects=True, vmem_limit_bytes=VMEM_LIMIT
        ),
        cost_estimate=pl.CostEstimate(
            flops=2 * seqs * length * width * depth, bytes_accessed=2 * depth * width, transcendentals=0
        ),
    )(mixed, w_out, own, gain)


def temporal_attention(packed, valid):
    length = packed.shape[0]
    packed = packed.reshape(length, -1, 3, HEAD)
    query = packed[:, :, 0]
    keys = packed[:, :, 1]
    values = packed[:, :, 2]
    scores = jnp.einsum(
        "ihe,jhe->hij", query, keys, preferred_element_type=jnp.float32
    ) / math.sqrt(HEAD)
    rows = lax.broadcasted_iota(jnp.int32, (length, length), 0)
    cols = lax.broadcasted_iota(jnp.int32, (length, length), 1)
    allowed = ((cols <= rows) & (cols < valid))[None]
    scores = jnp.where(allowed, scores, NEG)
    top = jnp.max(scores, axis=-1, keepdims=True)
    expo = jnp.where(allowed, jnp.exp(scores - top), 0.0)
    probs = (expo / jnp.sum(expo, axis=-1, keepdims=True)).astype(jnp.bfloat16)
    mixed = jnp.einsum("hij,jhe->ihe", probs, values, preferred_element_type=jnp.float32)
    return mixed.astype(jnp.bfloat16).reshape(length, -1)


def depth_attention(qkv):
    count, frames, width = qkv.shape
    inner = width // 3
    heads = inner // DHEAD
    query = qkv[:, :, :inner].astype(jnp.float32)
    keys = qkv[:, :, inner : 2 * inner].astype(jnp.float32)
    values = qkv[:, :, 2 * inner :].astype(jnp.float32)
    lane = lax.broadcasted_iota(jnp.int32, (inner, heads), 0) // DHEAD
    head = lax.broadcasted_iota(jnp.int32, (inner, heads), 1)
    seg = (lane == head).astype(jnp.bfloat16)
    prod = (query[:, None] * keys[None]).astype(jnp.bfloat16)
    score = jnp.einsum(
        "cnix,xh->cnih", prod, seg, preferred_element_type=jnp.float32
    ) / math.sqrt(DHEAD)
    mine = lax.broadcasted_iota(jnp.int32, (count, count, 1, 1), 0)
    other = lax.broadcasted_iota(jnp.int32, (count, count, 1, 1), 1)
    keep = other <= mine
    score = jnp.where(keep, score, NEG)
    top = jnp.max(score, axis=1, keepdims=True)
    expo = jnp.where(keep, jnp.exp(score - top), 0.0)
    probs = (expo / jnp.sum(expo, axis=1, keepdims=True)).astype(jnp.bfloat16)
    wide = jnp.einsum("cnih,xh->cnix", probs, seg, preferred_element_type=jnp.float32)
    return jnp.sum(wide * values[None], axis=1).astype(jnp.bfloat16)


def body(frames_in, valid_len, tokens, t_gain, w_qkv, w_out, h_gain, d_in, d_embed, d_gain, d_qkv):
    seqs = lax.axis_size("fsdp")
    parts = lax.axis_size("cb")
    own = frames_in[0]
    few = own.shape[0]
    packed = temporal_qkv(seqs, parts, own, t_gain[None], w_qkv)
    mixed = temporal_attention(packed, valid_len[0])
    hnorm = temporal_out(seqs, parts, mixed, w_out, own, h_gain[None])
    hnorm = hnorm.reshape(parts * few, -1)
    lifted = jnp.dot(hnorm, d_in[0], preferred_element_type=jnp.float32)
    lifted = lifted + jnp.take(d_embed[0], tokens[0, 0], axis=0).astype(jnp.float32)
    dnorm = rms_scale(lifted, d_gain[0]).astype(jnp.bfloat16)
    depth_all = jnp.dot(dnorm, d_qkv[0], preferred_element_type=jnp.float32).astype(jnp.bfloat16)
    depth_all = lax.all_to_all(depth_all, "cb", split_axis=0, concat_axis=0, tiled=True)
    result = depth_attention(depth_all.reshape(parts, few, -1))
    result = result.reshape(parts * few, -1)
    result = lax.all_to_all(result, "cb", split_axis=0, concat_axis=0, tiled=True)
    return result[None, None]


def solution(mesh):
    placed = (
        P("fsdp", "cb", None),
        P("fsdp"),
        P("fsdp", "cb", None),
        P(),
        P("fsdp", "cb"),
        P("cb", "fsdp"),
        P(),
        P("cb", None, None),
        P("cb", None, None),
        P("cb", None),
        P("cb", None, None),
    )
    return jax.shard_map(
        body, mesh=mesh, in_specs=placed, out_specs=P("fsdp", "cb", None, None), check_vma=False
    )
```

time: 585 us -> 238 us (0.41)
  waiting for transfers between devices: 410 us -> 21 us
  Pallas kernels: 0 us -> 174 us
  blocking collectives: 75.5 us -> 12.2 us
  local copies, waits for them, and re-layouts: 36.8 us -> 7.36 us
  other arithmetic: 20.3 us -> 0.59 us
  between operations: 14 us -> 0.83 us
  matrix products: 26.8 us -> 17.1 us
    all_gather x3 -> x0, waiting for transfers between devices: 205 us -> none  [the longest x1 114 us: body(): lax.all_gather(w_out, 'fsdp', axis=1, tiled=True)]
    pallas_call x0 -> x2, Pallas kernels: none -> 174 us  [the longest x1 99.9 us: temporal_qkv(): pl.pallas_call(functools.partial(qkv_kernel, seqs, chips), out_shape=jax....]
    reduce_scatter x1 -> x0, waiting for transfers between devices: 108 us -> none  [body(): lax.psum_scatter(jnp.dot(every, w_qkv, preferred_element_type=jnp.float32...]
    psum x1 -> x0, waiting for transfers between devices: 96.5 us -> none  [body(): total = lax.psum(partial_out, 'cb')]
    all_to_all x1, blocking collectives: 75.5 us -> 12.2 us  [body(): lax.all_to_all(result, 'cb', split_axis=0, concat_axis=0, tiled=True)]
    all_to_all x0 -> x1, waiting for transfers between devices: none -> 21 us  [body(): lax.all_to_all(depth_all, 'cb', split_axis=0, concat_axis=0, tiled=True)]
    unnamed x18 -> x9, local copies, waits for them, and re-layouts: 14.1 us -> 0.82 us
    dot_general x3, matrix products: 17.3 us -> 5.81 us  [the longest x1 2.82 us: depth_attention(): jnp.einsum('cnix,xh->cnih', prod, seg, preferred_element_type=jnp.float32)]
  transfers between devices with their start and end apart: 5 -> 1, of which waited for: 5 -> 1; matrix products, arithmetic and copies ran while one was open for 2% -> 0% of each run, Pallas kernels for 0% -> 0%
where the time goes in v1:
time: 238 us
  Pallas kernels  174 us (73%)
  waiting for transfers between devices  21 us (9%)
  matrix products  17.1 us (7%)
  blocking collectives  12.2 us (5%)
  local copies, waits for them, and re-layouts  7.36 us (3%)
  starting transfers between devices  4.58 us (2%)
    pallas_call x1, Pallas kernels, temporal_qkv(): pl.pallas_call(functools.partial(qkv_kernel, seqs, chips), out_shape=jax....  99.9 us
    pallas_call x1, Pallas kernels, temporal_out(): pl.pallas_call(functools.partial(out_kernel, seqs, chips), out_shape=jax....  74.3 us
    all_to_all x1, waiting for transfers between devices, body(): lax.all_to_all(depth_all, 'cb', split_axis=0, concat_axis=0, tiled=True)  21 us
    all_to_all x1, blocking collectives, body(): lax.all_to_all(result, 'cb', split_axis=0, concat_axis=0, tiled=True)  12.2 us
    dot_general x1, matrix products, body(): lifted = jnp.dot(hnorm, d_in[0], preferred_element_type=jnp.float32)  7.62 us
  transfers between devices with their start and end apart: 1, of which 1 were waited for; matrix products, arithmetic and copies ran while one was open for 0% of the time, Pallas kernels for 0%

profile of v1, /device:TPU:0, one launch (start us, length us, event | category | flops | bytes accessed | tf_op | source)
XLA Modules:
  0.0 237.8 jit_solution(14987713848637761905)
XLA Ops:
  0.0 99.9 %shard_map.109 = bf16[256,1536]{1,0:T(8,128)(2,1)} custom-call(bf16[32,6144]{1,0:T(8,128)(2,1)} %bitcast.81, f32[1,6144]{1,0:T(1,128)} %bitcast.83, bf16[1536,1536]{1,0:T(8,128)(2,1)} %w_hbm.1), custom_call_target="tpu_custom_call" | custom-call | flops 4831838208 | bytes 4718592 | tf_op jit(solution)/shard_map/pallas_call | solution.py:202
  99.9 1.4 copy.17
  101.9 0.1 fusion.26
  102.1 0.0 copy-start
  102.1 0.6 fusion.50
  102.7 0.8 convolution_convert_fusion
  103.5 0.8 copy.25.mixed
  104.4 0.0 copy-done
  104.4 4.3 %gather_fusion = bf16[256,1024]{1,0:T(8,128)(2,1)S(1)} fusion(bf16[2048,1024]{1,0:T(8,128)(2,1)} %bitcast.72, s32[1024]{0:T(1024)S(1)} %pad_clamp_fusion), kind=kCustom, calls=%fused_computation | custom fusion | bytes 1049600 | tf_op jit(solution)/shard_map/jit(_take)/gather | solution.py:443
  108.7 0.0 slice-start
  108.7 74.3 %shard_map.110 = bf16[8,32,6144]{2,1,0:T(8,128)(2,1)} custom-call(bf16[256,512]{1,0:T(8,128)(2,1)} %copy.25.mixed, bf16[512,1536]{1,0:T(8,128)(2,1)} %w.1, bf16[32,6144]{1,0:T(8,128)(2,1)} %bitcast.82, f32[1,6144]{1,0:T(1,128)} %bitcast.84), custom_call_target="tpu_custom_call" | custom-call | flops 1610612736 | bytes 1572864 | tf_op jit(solution)/shard_map/pallas_call | solution.py:356
  183.1 0.0 slice-start.1
  183.1 0.0 copy-start.1
  183.1 7.6 %multiply_reduce_fusion.1 = (f32[256]{0:T(256)S(1)}, f32[256,1024]{1,0:T(8,128)S(1)}) fusion(bf16[256,1024]{1,0:T(8,128)(2,1)S(1)} %gather_fusion, pred[256]{0:T(512)(128)(4,1)S(1)} %compare_and_fusion, bf16[256,6144]{1,0:T(8,128)(2,1)} %bitcast.86, bf16[1,6144,1024]{2,1,0:T(8,128)(2,1)} %param.18), kind=kOutput, calls=%fused_computation.22 | convolution fusion | flops 3222535936 | bytes 17302784 | tf_op jit(solution)/shard_map/dot_general | solution.py:442
  190.7 0.0 slice-done
  190.8 3.0 %fusion.8 = bf16[256,3072]{1,0:T(8,128)(2,1)} fusion(bf16[1,1024,3072]{2,1,0:T(8,128)(2,1)S(1)} %bitcast.80, f32[256,1024]{1,0:T(8,128)S(1)} %get-tuple-element.9, f32[1024]{0:T(1024)S(1)} %bitcast.85, f32[256]{0:T(256)S(1)} %add_rsqrt_fusion), kind=kOutput, calls=%fused_computation.11 | convolution fusion | flops 1612185600 | bytes 8918016 | tf_op jit(solution)/shard_map/dot_general | solution.py:445
  193.8 4.6 %all-to-all-start = ((bf16[8,32,3072]{2,1,0:T(8,128)(2,1)}), bf16[8,32,3072]{2,1,0:T(8,128)(2,1)S(1)}, u32[]{:S(2)}, u32[]{:S(2)}) async-start(bf16[8,32,3072]{2,1,0:T(8,128)(2,1)} %bitcast.18), calls=%async_computation | async-start | bytes 3145728 | tf_op jit(solution)/shard_map/all_to_all | solution.py:446
  198.4 21.0 %all-to-all-done = bf16[8,32,3072]{2,1,0:T(8,128)(2,1)S(1)} async-done(((bf16[8,32,3072]{2,1,0:T(8,128)(2,1)}), bf16[8,32,3072]{2,1,0:T(8,128)(2,1)S(1)}, u32[]{:S(2)}, u32[]{:S(2)}) %all-to-all-start) | async-done | bytes 1572896 | tf_op jit(solution)/shard_map/all_to_all | solution.py:446
  219.4 0.3 slice_convert_fusion.2
  219.7 2.8 %fusion.51 = (f32[8,32,16]{1,2,0:T(8,128)S(1)}, f32[8,8,32,16]{2,3,1,0:T(8,128)S(1)}) fusion(s32[1024]{0:T(1024)S(1)} %get-tuple-element.12, s32[1024]{0:T(1024)S(1)} %get-tuple-element.13, pred[1024]{0:T(1024)(128)(4,1)S(1)} %fusion.39, f32[8,32,1024]{2,1,0:T(8,128)S(1)} %get-tuple-element.7, f32[8,32,1024]{2,1,0:T(8,128)S(1)} %get-tuple-element.5, ...), kind=kOutput, calls=%fused_computation.72 | convolution fusion | flops 71430144 | bytes 2253888 | tf_op jit(solution)/shard_map/cnix,xh->cnih/dot_general | solution.py:419
  222.5 0.2 fusion.22
  222.7 2.2 multiply_reduce_fusion
  224.9 12.2 %all_to_all.15 = bf16[8,32,1024]{2,1,0:T(8,128)(2,1)S(1)} all-to-all(bf16[8,32,1024]{2,1,0:T(8,128)(2,1)S(1)} %multiply_reduce_fusion), channel_id=1, replica_groups=mesh['fsdp'=4,'cb'=8] {'cb'}, dimensions={0} | all-to-all | bytes 1048576 | tf_op jit(solution)/shard_map/all_to_all | solution.py:449
  237.0 0.8 copy.31
  (11 shorter events, 0.1 us)
Async XLA Ops:
  102.1 2.3 copy-start
  108.7 82.0 %slice-start = ((s8[6291456]{0:T(1024)(128)(4,1)}), s8[2097152]{0:T(1024)(128)(4,1)S(1)}, s32[]{:S(2)}) async-start(s8[6291456]{0:T(1024)(128)(4,1)} %bitcast.79), calls=%async_computation.2 | async-start | bytes 4194304
  183.1 7.7 %slice-start.1 = ((s8[6291456]{0:T(1024)(128)(4,1)}), s8[4194304]{0:T(1024)(128)(4,1)S(1)}, s32[]{:S(2)}) async-start(s8[6291456]{0:T(1024)(128)(4,1)} %bitcast.79), calls=%async_computation.3 | async-start | bytes 8388608
  183.1 7.7 %copy-start.1 = (f32[1,1024]{1,0:T(1,128)S(1)}, f32[1,1024]{1,0:T(1,128)}, u32[]{:S(2)}) copy-start(f32[1,1024]{1,0:T(1,128)} %param.20) | copy-start | bytes 12292
  193.8 25.6 %all-to-all-start = ((bf16[8,32,3072]{2,1,0:T(8,128)(2,1)}), bf16[8,32,3072]{2,1,0:T(8,128)(2,1)S(1)}, u32[]{:S(2)}, u32[]{:S(2)}) async-start(bf16[8,32,3072]{2,1,0:T(8,128)(2,1)} %bitcast.18), calls=%async_computation | async-start | bytes 3145728 | tf_op jit(solution)/shard_map/all_to_all | solution.py:446

commit v2 on v1

--- a/solution.py
+++ b/solution.py
@@ -16,13 +16,17 @@
 NEG = -1e30
 
 
-def rms_scale(values, gain):
-    mean_sq = jnp.mean(values * values, axis=-1, keepdims=True)
-    return values * lax.rsqrt(mean_sq + EPS) * gain
-
-
 MESH = pl.DeviceIdType.MESH
 VMEM_LIMIT = 56 * 1024 * 1024
+
+
+def full_barrier(seqs, parts, f, me):
+    barrier = pltpu.get_barrier_semaphore()
+    for d in range(1, seqs):
+        pl.semaphore_signal(barrier, inc=1, device_id={"fsdp": lax.rem(f + d, seqs)}, device_id_type=MESH)
+    for e in range(1, parts):
+        pl.semaphore_signal(barrier, inc=1, device_id={"cb": lax.rem(me + e, parts)}, device_id_type=MESH)
+    pl.semaphore_wait(barrier, seqs + parts - 2)
 
 
 def entry_barrier(seqs, chips, f, chip, core):
@@ -89,7 +93,7 @@
         source = lax.rem(chip - e + chips, chips) * 2 + core
         return send(gat.at[source, s], gat.at[source, s], b_send.at[s, e], b_recv.at[s, e], {"cb": sibling})
 
-    for s in order:
+    def push(s):
         @pl.when(s != f)
         def _():
             send(normed.at[s], gat.at[me, s], z_send.at[s], z_recv.at[s], {"fsdp": s}).wait_recv()
@@ -98,15 +102,20 @@
             to_chip(s, e).start()
         to_sibling(s, 0).start()
 
+    push(order[0])
+
     def to_right(t):
         return send(part.at[t], from_left.at[t], right_send.at[t], right_recv.at[t], {"fsdp": lax.rem(f + 1, seqs)})
 
     def to_left(t):
         return send(part.at[t], from_right.at[t], left_send.at[t], left_recv.at[t], {"fsdp": lax.rem(f + last, seqs)})
 
-    load.wait()
     tile = 256
-    for s in order:
+    for k, s in enumerate(order):
+        if k + 1 < seqs:
+            for e in range(1, chips):
+                to_chip(s, e).wait_send()
+            push(order[k + 1])
         for e in range(1, chips):
             source = lax.rem(chip - e + chips, chips) * 2 + core
             send(gat.at[source, s], gat.at[source, s], c_send.at[s, e], c_recv.at[s, e], {"cb": sibling}).wait_recv()
@@ -115,6 +124,9 @@
             source = lax.rem(chip - e + chips, chips) * 2 + 1 - core
             send(gat.at[source, s], gat.at[source, s], b_send.at[s, e], b_recv.at[s, e], {"cb": sibling}).wait_recv()
 
+        if k == 0:
+            load.wait()
+
         def multiply(step, carry):
             at = pl.ds(pl.multiple_of(step * tile, tile), tile)
             lhs = gat[:, s].reshape(length, width)
@@ -122,14 +134,26 @@
             return carry
 
         lax.fori_loop(0, cols // tile, multiply, 0)
-        if s > 0:
+        if s == last:
             @pl.when(f == 0)
             def _():
                 to_right(s).start()
-        if s < last:
+        if s == 0:
             @pl.when(f == last)
             def _():
                 to_left(s).start()
+
+    @pl.when(f == 0)
+    def _():
+        for t in range(last - 1, 0, -1):
+            to_right(t + 1).wait_send()
+            to_right(t).start()
+
+    @pl.when(f == last)
+    def _():
+        for u in range(1, last):
+            to_left(u - 1).wait_send()
+            to_left(u).start()
 
     def add(target, t, other):
         def rows(step, carry):
@@ -178,17 +202,17 @@
         def _():
             along_z(s).wait_send()
 
-        @pl.when(s > f)
+        @pl.when((s > f) & ((f > 0) | (s == 1)))
         def _():
             to_right(s).wait_send()
 
-        @pl.when(s < f)
+        @pl.when((s < f) & ((f < last) | (s == last - 1)))
         def _():
             to_left(s).wait_send()
 
         for e in range(chips):
             to_sibling(s, e).wait_send()
-            if e > 0:
+            if e > 0 and s == order[-1]:
                 to_chip(s, e).wait_send()
 
 
@@ -227,8 +251,11 @@
 
 
 def out_kernel(
-    seqs, chips, mixed, w, own, gain, out, gath, part, from_sib, acc, from_chip, total, cols, hid, gat,
-    z_send, z_recv, s_send, s_recv, c_send, c_recv, t_send, t_recv, g_send, g_recv, b_send, b_recv, o_sem,
+    seqs, chips, mixed, w, own, gain, ids, d_gain, d_in_hbm, table_hbm, d_qkv_hbm, out,
+    gath, part, from_sib, acc, from_chip, total, cols, hid, gat, d_in, table, d_qkv, lifted, dnorm, mine, theirs,
+    done, back,
+    z_send, z_recv, s_send, s_recv, c_send, c_recv, t_send, t_recv, g_send, g_recv, b_send, b_recv,
+    a_send, a_recv, r_send, r_recv, w_sem,
 ):
     f = lax.axis_index("fsdp")
     me = lax.axis_index("cb")
@@ -238,7 +265,16 @@
     width = wide // seqs
     length = mixed.shape[0]
     tile = 256
-    entry_barrier(seqs, chips, f, chip, core)
+    parts = 2 * chips
+    inner = lifted.shape[1]
+    loads = [
+        pltpu.make_async_copy(table_hbm, table, w_sem.at[0]),
+        pltpu.make_async_copy(d_in_hbm, d_in, w_sem.at[1]),
+        pltpu.make_async_copy(d_qkv_hbm, d_qkv, w_sem.at[2]),
+    ]
+    for load in loads:
+        load.start()
+    full_barrier(seqs, parts, f, me)
 
     def along_z(d):
         return send(mixed, gath.at[f], z_send.at[d], z_recv.at[d], {"fsdp": lax.rem(f + d, seqs)})
@@ -273,7 +309,19 @@
         lax.fori_loop(0, width // tile, multiply, 0)
         to_sibling(s, d).start()
 
-    for d in range(seqs):
+    loads[0].wait()
+    entries = table.shape[0]
+
+    def lookup_tile(step, carry):
+        at = pl.ds(pl.multiple_of(step * tile, tile), tile)
+        spread = lax.broadcasted_iota(jnp.int32, (length, entries), 1)
+        hot = jnp.where(spread == ids[...], 1.0, 0.0).astype(jnp.bfloat16)
+        lifted[:, at] = jnp.dot(hot, table[:, at], preferred_element_type=jnp.float32)
+        return carry
+
+    turns = list(range(1, seqs)) + [0]
+
+    def reduce_pair(d):
         s = lax.rem(f - d + seqs, seqs)
         to_sibling(s, d).wait_recv()
 
@@ -287,8 +335,15 @@
         for e in range(1, chips):
             to_chip(s, d, e).start()
 
-    for d in range(seqs):
+    reduce_pair(turns[0])
+    for k, d in enumerate(turns):
         s = lax.rem(f - d + seqs, seqs)
+        if k + 1 < seqs:
+            for e in range(1, chips):
+                to_chip(s, d, e).wait_send()
+            reduce_pair(turns[k + 1])
+        else:
+            lax.fori_loop(0, inner // tile, lookup_tile, 0)
         value = acc[s, chip].astype(jnp.float32)
         for e in range(1, chips):
             to_chip(s, d, e).wait_recv()
@@ -328,13 +383,90 @@
         forward(e).start()
     for e in range(chips):
         forward(e).wait_recv()
-    keep = pltpu.make_async_copy(gat, out, o_sem)
-    keep.start()
+    loads[1].wait()
+
+    def lift(step, carry):
+        at = pl.ds(pl.multiple_of(step * tile, tile), tile)
+        lifted[:, at] += jnp.dot(gat[...].reshape(length, wide), d_in[:, at], preferred_element_type=jnp.float32)
+        return carry
+
+    lax.fori_loop(0, inner // tile, lift, 0)
+
+    def norm_rows(step, carry):
+        at = pl.ds(pl.multiple_of(step * 32, 32), 32)
+        rows = lifted[at]
+        mean = jnp.sum(rows * rows, axis=-1, keepdims=True) / inner
+        dnorm[at] = (rows * lax.rsqrt(mean + EPS) * d_gain[...]).astype(jnp.bfloat16)
+        return carry
+
+    lax.fori_loop(0, length // 32, norm_rows, 0)
+
+    def scatter(third, e):
+        to = lax.rem(me + e, parts)
+        return send(mine.at[third, to], theirs.at[third, me], a_send.at[third, e], a_recv.at[third, e], {"cb": to})
+
+    loads[2].wait()
+    for third in range(3):
+        def project(step, carry):
+            at = pl.ds(pl.multiple_of(step * tile, tile), tile)
+            source = pl.ds(pl.multiple_of(third * inner + step * tile, tile), tile)
+            value = jnp.dot(dnorm[...], d_qkv[:, source], preferred_element_type=jnp.float32).astype(jnp.bfloat16)
+            mine[third, :, :, at] = value.reshape(parts, few, tile)
+            return carry
+
+        lax.fori_loop(0, inner // tile, project, 0)
+        for e in range(1, parts):
+            scatter(third, e).start()
+        theirs[third, me] = mine[third, me]
+    lane = lax.broadcasted_iota(jnp.int32, (inner, 128), 0) // DHEAD
+    head = lax.broadcasted_iota(jnp.int32, (inner, 128), 1)
+    seg = jnp.where(lane == head, 1.0, 0.0).astype(jnp.bfloat16)
+    lane = lax.broadcasted_iota(jnp.int32, (128, inner), 1) // DHEAD
+    head = lax.broadcasted_iota(jnp.int32, (128, inner), 0)
+    spread = jnp.where(lane == head, 1.0, 0.0).astype(jnp.bfloat16)
+    for third in range(3):
+        for e in range(1, parts):
+            scatter(third, e).wait_recv()
+
+    def attend(c):
+        query = theirs[0, c].astype(jnp.float32)
+        prod = (theirs[1].astype(jnp.float32) * query[None]).astype(jnp.bfloat16)
+        score = jnp.dot(prod.reshape(length, inner), seg, preferred_element_type=jnp.float32)
+        score = score.reshape(parts, few, 128) * (1.0 / math.sqrt(DHEAD))
+        keep = lax.broadcasted_iota(jnp.int32, (parts, few, 128), 0) <= c
+        score = jnp.where(keep, score, NEG)
+        top = jnp.max(score, axis=0, keepdims=True)
+        expo = jnp.where(keep, jnp.exp(score - top), 0.0)
+        probs = (expo / jnp.sum(expo, axis=0, keepdims=True)).astype(jnp.bfloat16)
+        full = jnp.dot(probs.reshape(length, 128), spread, preferred_element_type=jnp.float32)
+        full = full.reshape(parts, few, inner) * theirs[2].astype(jnp.float32)
+        return jnp.sum(full, axis=0).astype(jnp.bfloat16)
+
+    def give(e):
+        to = lax.rem(me + e, parts)
+        return send(done.at[to], back.at[me], r_send.at[e], r_recv.at[e], {"cb": to})
+
+    def each(e, carry):
+        c = lax.rem(me + e, parts)
+        done[c] = attend(c)
+        give(e).start()
+        return carry
+
+    lax.fori_loop(1, parts, each, 0)
+    back[me] = attend(me)
+    for e in range(1, parts):
+        give(e).wait_recv()
+    out[...] = back[...]
+    for e in range(1, parts):
+        give(e).wait_send()
+        for third in range(3):
+            scatter(third, e).wait_send()
     for d in range(seqs):
         s = lax.rem(f - d + seqs, seqs)
         to_sibling(s, d).wait_send()
-        for e in range(1, chips):
-            to_chip(s, d, e).wait_send()
+        if d == turns[-1]:
+            for e in range(1, chips):
+                to_chip(s, d, e).wait_send()
         if d > 0:
             along_z(d).wait_send()
             to_seq(s, d).wait_send()
@@ -342,12 +474,12 @@
         forward(e).wait_send()
         if e > 0:
             share(e).wait_send()
-    keep.wait()
-
-
-def temporal_out(seqs, parts, mixed, w_out, own, gain):
+
+
+def out_and_depth(seqs, parts, mixed, w_out, own, gain, ids, d_gain, d_in, table, d_qkv):
     few, wide = own.shape
     depth, width = w_out.shape
+    inner = d_in.shape[1]
     chips = parts // 2
     length = parts * few
     dma = pltpu.SemaphoreType.DMA
@@ -355,9 +487,9 @@
     bf16 = jnp.bfloat16
     return pl.pallas_call(
         functools.partial(out_kernel, seqs, chips),
-        out_shape=jax.ShapeDtypeStruct((parts, few, wide), bf16),
-        in_specs=[vmem] * 4,
-        out_specs=pl.BlockSpec(memory_space=pl.ANY),
+        out_shape=jax.ShapeDtypeStruct((parts, few, inner), bf16),
+        in_specs=[vmem] * 6 + [pl.BlockSpec(memory_space=pl.ANY)] * 3,
+        out_specs=vmem,
         scratch_shapes=[
             pltpu.VMEM((seqs, length, depth), bf16),
             pltpu.VMEM((2, seqs, chips, few, width), bf16),
@@ -368,13 +500,24 @@
             pltpu.VMEM((seqs, few, width), bf16),
             pltpu.VMEM((few, wide), jnp.float32),
             pltpu.VMEM((parts, few, wide), bf16),
+            pltpu.VMEM(d_in.shape, bf16),
+            pltpu.VMEM(table.shape, bf16),
+            pltpu.VMEM(d_qkv.shape, bf16),
+            pltpu.VMEM((length, inner), jnp.float32),
+            pltpu.VMEM((length, inner), bf16),
+            pltpu.VMEM((3, parts, few, inner), bf16),
+            pltpu.VMEM((3, parts, few, inner), bf16),
+            pltpu.VMEM((parts, few, inner), bf16),
+            pltpu.VMEM((parts, few, inner), bf16),
             dma((seqs,)), dma((seqs,)),
             dma((seqs,)), dma((seqs,)),
             dma((seqs, chips)), dma((seqs, chips)),
             dma((seqs,)), dma((seqs,)),
             dma((chips,)), dma((chips,)),
             dma((chips,)), dma((chips,)),
-            dma,
+            dma((3, parts)), dma((3, parts)),
+            dma((parts,)), dma((parts,)),
+            dma((3,)),
         ],
         compiler_params=pltpu.CompilerParams(
             collective_id=1, has_side_effects=True, vmem_limit_bytes=VMEM_LIMIT
@@ -382,7 +525,7 @@
         cost_estimate=pl.CostEstimate(
             flops=2 * seqs * length * width * depth, bytes_accessed=2 * depth * width, transcendentals=0
         ),
-    )(mixed, w_out, own, gain)
+    )(mixed, w_out, own, gain, ids, d_gain, d_in, table, d_qkv)
 
 
 def temporal_attention(packed, valid):
@@ -405,31 +548,6 @@
     return mixed.astype(jnp.bfloat16).reshape(length, -1)
 
 
-def depth_attention(qkv):
-    count, frames, width = qkv.shape
-    inner = width // 3
-    heads = inner // DHEAD
-    query = qkv[:, :, :inner].astype(jnp.float32)
-    keys = qkv[:, :, inner : 2 * inner].astype(jnp.float32)
-    values = qkv[:, :, 2 * inner :].astype(jnp.float32)
-    lane = lax.broadcasted_iota(jnp.int32, (inner, heads), 0) // DHEAD
-    head = lax.broadcasted_iota(jnp.int32, (inner, heads), 1)
-    seg = (lane == head).astype(jnp.bfloat16)
-    prod = (query[:, None] * keys[None]).astype(jnp.bfloat16)
-    score = jnp.einsum(
-        "cnix,xh->cnih", prod, seg, preferred_element_type=jnp.float32
-    ) / math.sqrt(DHEAD)
-    mine = lax.broadcasted_iota(jnp.int32, (count, count, 1, 1), 0)
-    other = lax.broadcasted_iota(jnp.int32, (count, count, 1, 1), 1)
-    keep = other <= mine
-    score = jnp.where(keep, score, NEG)
-    top = jnp.max(score, axis=1, keepdims=True)
-    expo = jnp.where(keep, jnp.exp(score - top), 0.0)
-    probs = (expo / jnp.sum(expo, axis=1, keepdims=True)).astype(jnp.bfloat16)
-    wide = jnp.einsum("cnih,xh->cnix", probs, seg, preferred_element_type=jnp.float32)
-    return jnp.sum(wide * values[None], axis=1).astype(jnp.bfloat16)
-
-
 def body(frames_in, valid_len, tokens, t_gain, w_qkv, w_out, h_gain, d_in, d_embed, d_gain, d_qkv):
     seqs = lax.axis_size("fsdp")
     parts = lax.axis_size("cb")
@@ -437,16 +555,10 @@
     few = own.shape[0]
     packed = temporal_qkv(seqs, parts, own, t_gain[None], w_qkv)
     mixed = temporal_attention(packed, valid_len[0])
-    hnorm = temporal_out(seqs, parts, mixed, w_out, own, h_gain[None])
-    hnorm = hnorm.reshape(parts * few, -1)
-    lifted = jnp.dot(hnorm, d_in[0], preferred_element_type=jnp.float32)
-    lifted = lifted + jnp.take(d_embed[0], tokens[0, 0], axis=0).astype(jnp.float32)
-    dnorm = rms_scale(lifted, d_gain[0]).astype(jnp.bfloat16)
-    depth_all = jnp.dot(dnorm, d_qkv[0], preferred_element_type=jnp.float32).astype(jnp.bfloat16)
-    depth_all = lax.all_to_all(depth_all, "cb", split_axis=0, concat_axis=0, tiled=True)
-    result = depth_attention(depth_all.reshape(parts, few, -1))
+    result = out_and_depth(
+        seqs, parts, mixed, w_out, own, h_gain[None], tokens[0, 0][:, None], d_gain, d_in[0], d_embed[0], d_qkv[0]
+    )
     result = result.reshape(parts * few, -1)
-    result = lax.all_to_all(result, "cb", split_axis=0, concat_axis=0, tiled=True)
     return result[None, None]
 
 

time: 238 us -> 208 us (0.87)
  Pallas kernels: 174 us -> 199 us
  waiting for transfers between devices: 21 us -> 0 us
  matrix products: 17.1 us -> 1.46 us
  blocking collectives: 12.2 us -> 0 us
  starting transfers between devices: 4.58 us -> 0 us
  local copies, waits for them, and re-layouts: 7.36 us -> 4.92 us
    pallas_call x1, Pallas kernels: 74.3 us -> 101 us  [out_and_depth(): pl.pallas_call(functools.partial(out_kernel, seqs, chips), out_shape=jax....]
    all_to_all x1 -> x0, waiting for transfers between devices: 21 us -> none  [body(): lax.all_to_all(depth_all, 'cb', split_axis=0, concat_axis=0, tiled=True)]
    dot_general x4 -> x0, matrix products: 15.6 us -> none  [the longest x1 7.62 us: body(): lifted = jnp.dot(hnorm, d_in[0], preferred_element_type=jnp.float32)]
    all_to_all x1 -> x0, blocking collectives: 12.2 us -> none  [body(): lax.all_to_all(result, 'cb', split_axis=0, concat_axis=0, tiled=True)]
    all_to_all x1 -> x0, starting transfers between devices: 4.58 us -> none  [body(): lax.all_to_all(depth_all, 'cb', split_axis=0, concat_axis=0, tiled=True)]
    gather x1 -> x0, local copies, waits for them, and re-layouts: 4.29 us -> none  [body(): jnp.take(d_embed[0], tokens[0, 0], axis=0).astype(jnp.float32)]
  transfers between devices with their start and end apart: 1 -> 0, of which waited for: 1 -> 0; matrix products, arithmetic and copies ran while one was open for 0% -> 0% of each run, Pallas kernels for 0% -> 0%
where the time goes in v2:
time: 208 us; the launch traced here: 207 us
  Pallas kernels  199 us (96%)
  local copies, waits for them, and re-layouts  4.92 us (2%)
    pallas_call x1, Pallas kernels, out_and_depth(): pl.pallas_call(functools.partial(out_kernel, seqs, chips), out_shape=jax....  101 us
    pallas_call x1, Pallas kernels, temporal_qkv(): pl.pallas_call(functools.partial(qkv_kernel, seqs, chips), out_shape=jax....  98.3 us

profile of v2, /device:TPU:0, one launch (start us, length us, event | category | flops | bytes accessed | tf_op | source)
XLA Modules:
  0.0 206.7 jit_solution(4753846262814456783)
XLA Ops:
  0.0 98.3 %shard_map.109 = bf16[256,1536]{1,0:T(8,128)(2,1)} custom-call(bf16[32,6144]{1,0:T(8,128)(2,1)} %bitcast.53, f32[1,6144]{1,0:T(1,128)} %bitcast.58, bf16[1536,1536]{1,0:T(8,128)(2,1)} %w_hbm.1), custom_call_target="tpu_custom_call" | custom-call | flops 4831838208 | bytes 4718592 | tf_op jit(solution)/shard_map/pallas_call | solution.py:226
  98.3 1.4 copy.17
  100.4 0.1 fusion.5
  100.5 0.0 copy-start
  100.5 0.6 fusion.15
  101.1 0.8 convolution_convert_fusion
  102.0 0.8 copy.25.mixed
  102.8 0.0 copy-done
  102.8 0.8 copy.23.ids
  103.6 101.2 %shard_map.110 = bf16[8,32,1024]{2,1,0:T(8,128)(2,1)} custom-call(bf16[256,512]{1,0:T(8,128)(2,1)} %copy.25.mixed, bf16[512,1536]{1,0:T(8,128)(2,1)} %w.1, bf16[32,6144]{1,0:T(8,128)(2,1)} %bitcast.54, f32[1,6144]{1,0:T(1,128)} %bitcast.56, s32[256,1]{1,0:T(8,128)} %copy.23.ids, f32[1,1024]{1,0:T(1,128)} %d_gain.1, bf16[6144,1024]{1,0:T(8,128)(2,1)} %bitcast.47, ...), custom_call_target="tpu_custom_call" | custom-call | flops 1610612736 | bytes 1572864 | tf_op jit(solution)/shard_map/pallas_call | solution.py:488
  204.8 1.9 copy.31
  (1 shorter events, 0.0 us)
Async XLA Ops:
  100.5 2.3 %copy-start = (s32[1,1,256]{2,1,0:T(1,128)S(1)}, s32[1,1,256]{2,1,0:T(1,128)}, u32[]{:S(2)}) copy-start(s32[1,1,256]{2,1,0:T(1,128)} %param.13) | copy-start | bytes 3076
